TPU v7x, 32 devices: a whole 2x2x4 slice. The times are simulated.
32 devices in a mesh: group: 2 (over x), row: 16 (over z, y, core), col: 1.
Axes of the slice: x: 2, y: 2, z: 4, core: 2. Of those that a mesh axis runs over, the one named last changes fastest.
Arguments:
- pair: bfloat16 [256, 128, 128], P(('group', 'row'), 'col'), parts along dimension 0, may hold values from -6 to 6
- residue_mask: int32 [256], P('group'), parts along dimension 0, may hold values 0 or 1
- ln_gain: float32 [2, 128], replicated, may hold values from 0.1 to 1.9
- ln_bias: float32 [2, 128], replicated, may hold values from -0.45 to 0.45
- w_ab: bfloat16 [2, 128, 512], replicated, may hold values from -0.5 to 0.5
- w_gate: bfloat16 [2, 128, 128], replicated, may hold values from -0.5 to 0.5
- out_gain: float32 [2, 128], replicated, may hold values from 1.3 to 2.2
- out_bias: float32 [2, 128], replicated, may hold values from -1 to 1
- w_out: bfloat16 [2, 128, 128], replicated, may hold values from -0.110485435 to 0.110485435
Outputs:
- updated: bfloat16 [256, 128, 128], P(('group', 'row'), 'col'), parts along dimension 0
There are 2 independent parts, one for each index of `group`. A program takes and returns all parts, laid end to end along the dimension named above; an argument that names none is the same for every part. Nothing has to cross between parts.
All inputs are finite; a program needn't handle non-finite values.
Results may differ from a plain program's by a relative error of at most 0.019.
Values may be sent and summed in bfloat16 or wider, within the bound.
A program may use at most 128 MiB of HBM per device.

v0:
```python
import functools

import jax
import jax.numpy as jnp
from jax import lax
from jax.experimental import pallas as pl
from jax.experimental.pallas import tpu as pltpu
from jax.sharding import PartitionSpec as P


def from_root(value, axis, source):
    kept = jnp.where(lax.axis_index(axis) == source, value, 0).astype(value.dtype)
    return lax.psum(kept, axis)


def layer_norm(v, gain, bias):
    mean = jnp.mean(v, axis=-1, keepdims=True)
    centred = v - mean
    var = jnp.mean(centred * centred, axis=-1, keepdims=True)
    return centred * lax.rsqrt(var + 1e-05) * gain + bias


def project(z, pm, layer, ln_gain, ln_bias, w_ab, w_gate):
    rows, cols, chans = z.shape
    hidden = w_ab.shape[2] // 4
    zn = layer_norm(z.astype(jnp.float32), ln_gain[layer], ln_bias[layer]).astype(jnp.bfloat16)
    flat = zn.reshape(rows * cols, chans)
    proj = jnp.dot(flat, w_ab[layer], preferred_element_type=jnp.float32).reshape(
        rows, cols, 4 * hidden
    )
    mask3 = pm[:, :, None]
    left = (jax.nn.sigmoid(proj[..., :hidden]) * proj[..., hidden : 2 * hidden] * mask3).astype(
        jnp.bfloat16
    )
    right = (
        jax.nn.sigmoid(proj[..., 2 * hidden : 3 * hidden]) * proj[..., 3 * hidden :] * mask3
    ).astype(jnp.bfloat16)
    gate = jax.nn.sigmoid(jnp.dot(flat, w_gate[layer], preferred_element_type=jnp.float32)).reshape(
        rows, cols, chans
    )
    return (left, right, gate)


def finish(z, x, gate, layer, out_gain, out_bias, w_out):
    rows, cols, chans = z.shape
    hidden = x.shape[2]
    xn = layer_norm(x, out_gain[layer], out_bias[layer]).astype(jnp.bfloat16)
    delta = jnp.dot(
        xn.reshape(rows * cols, hidden), w_out[layer], preferred_element_type=jnp.float32
    )
    return (z.astype(jnp.float32) + gate * delta.reshape(rows, cols, chans)).astype(jnp.bfloat16)


def shards(pair, residue_mask, ln_gain, ln_bias, w_ab, w_gate, out_gain, out_bias, w_out):
    rows, cols, chans = pair.shape
    hidden = w_out.shape[1]
    row_count = lax.axis_size("row")
    total = rows * row_count
    row_pos = lax.axis_index("row")
    col_pos = lax.axis_index("col")
    maskf = residue_mask.astype(jnp.float32)
    mask_rows = lax.dynamic_slice_in_dim(maskf, row_pos * rows, rows)
    mask_cols = lax.dynamic_slice_in_dim(maskf, col_pos * cols, cols)
    pm = mask_rows[:, None] * mask_cols[None, :]
    left, right, gate = project(pair, pm, 0, ln_gain, ln_bias, w_ab, w_gate)
    left_flat = left.reshape(rows, cols * hidden)
    right_flat = right.reshape(rows, cols * hidden)
    left_wide, right_wide = (
        lax.all_gather(left_flat, "col", axis=1, tiled=True),
        lax.all_gather(right_flat, "col", axis=1, tiled=True),
    )
    left_full = left_wide.reshape(rows, total, hidden)
    piece = lax.all_gather(right_wide, "row", axis=0, tiled=True)
    count = piece.shape[0]
    contrib = jnp.einsum(
        "ikc,jkc->ijc",
        left_full,
        piece.reshape(count, total, hidden),
        preferred_element_type=jnp.float32,
    )
    outgoing = lax.dynamic_slice_in_dim(contrib, col_pos * cols, cols, 1)
    first = finish(pair, outgoing, gate, 0, out_gain, out_bias, w_out)
    left, right, gate = project(first, pm, 1, ln_gain, ln_bias, w_ab, w_gate)
    blocks_half = cols // rows
    left_blocks = left.reshape(rows, blocks_half, rows * hidden)
    padded = jnp.zeros((rows, row_count, rows * hidden), jnp.bfloat16)
    padded = lax.dynamic_update_slice_in_dim(padded, left_blocks, col_pos * blocks_half, 1)
    received = lax.all_to_all(padded, "row", split_axis=1, concat_axis=0, tiled=True)
    owner = row_pos * rows // cols
    left_cols = from_root(received, "col", owner).reshape(total, rows, hidden)
    piece = lax.all_gather(right.reshape(rows, cols * hidden), "row", axis=0, tiled=True)
    count = piece.shape[0]
    incoming = jnp.einsum(
        "kic,kjc->ijc",
        left_cols,
        piece.reshape(count, cols, hidden),
        preferred_element_type=jnp.float32,
    )
    return finish(first, incoming, gate, 1, out_gain, out_bias, w_out)


F32 = jnp.float32
BF16 = jnp.bfloat16
TILE = 8
LANES = 128


def sigmoid(v):
    return 0.5 * jnp.tanh(0.5 * v) + 0.5


def matmul(a, b, contract=((1,), (0,))):
    return lax.dot_general(a, b, (contract, ((), ())), preferred_element_type=F32)


def column(ref, layer):
    row = ref[layer : layer + 1, :]
    return jnp.transpose(jnp.broadcast_to(row, (row.shape[1], row.shape[1])))


def fused(
    count,
    pair_ref,
    mask_ref,
    mask_s,
    ln_gain,
    ln_bias,
    w_ab,
    w_gate,
    out_gain,
    out_bias,
    w_out,
    out_ref,
    z_t,
    zn_t,
    gate_t,
    stage,
    lr_out,
    lr_in,
    x_out,
    x_in,
    x_wide,
    lr_send,
    lr_recv,
    x_send,
    x_recv,
):
    rows, n, chans = pair_ref.shape
    hidden = w_out.shape[1]
    own = hidden // count
    per_lr = 2 * rows
    me = lax.axis_index("row")

    barrier = pltpu.get_barrier_semaphore()

    def greet(step, carry):
        other = lax.rem(me + step, count)
        pl.semaphore_signal(
            barrier, inc=1, device_id={"row": other}, device_id_type=pl.DeviceIdType.MESH
        )
        return carry

    lax.fori_loop(1, count, greet, 0)

    def lr_copy(u, slot_out, slot_in, other):
        return pltpu.make_async_remote_copy(
            src_ref=lr_out.at[u, slot_out],
            dst_ref=lr_in.at[u, slot_in],
            send_sem=lr_send.at[u, slot_out],
            recv_sem=lr_recv.at[u, slot_in],
            device_id={"row": other},
            device_id_type=pl.DeviceIdType.MESH,
        )

    def x_copy(u, slot_out, slot_in, other):
        return pltpu.make_async_remote_copy(
            src_ref=x_out.at[u, slot_out],
            dst_ref=x_in.at[u, slot_in],
            send_sem=x_send.at[u, slot_out],
            recv_sem=x_recv.at[u, slot_in],
            device_id={"row": other},
            device_id_type=pl.DeviceIdType.MESH,
        )

    mask_k = mask_ref[...].astype(F32)
    for i in range(rows):
        z_t[i] = jnp.transpose(pair_ref[i].astype(F32))

    for u in range(2):
        w_t = jnp.transpose(w_ab[u].astype(F32)).astype(BF16)
        gain, bias = column(ln_gain, u), column(ln_bias, u)
        for i in range(rows):
            z = z_t[i]
            mean = jnp.mean(z, axis=0, keepdims=True)
            centred = z - mean
            var = jnp.mean(centred * centred, axis=0, keepdims=True)
            zn = (centred * lax.rsqrt(var + 1e-05) * gain + bias).astype(BF16)
            zn_t[i] = zn
            proj = matmul(w_t, zn)
            pm = mask_k * mask_s[me * rows + i].astype(F32)
            left = sigmoid(proj[:hidden]) * proj[hidden : 2 * hidden] * pm
            right = sigmoid(proj[2 * hidden : 3 * hidden]) * proj[3 * hidden :] * pm
            stage[pl.ds(i, hidden, stride=per_lr), :] = left
            stage[pl.ds(rows + i, hidden, stride=per_lr), :] = right

        if u == 0:
            pl.semaphore_wait(barrier, count - 1)

        def lr_start(step, carry):
            other = lax.rem(me + step, count)
            begin = pl.multiple_of(other * (own * per_lr), own * per_lr)
            lr_out[u, other] = stage[pl.ds(begin, own * per_lr), :].astype(BF16)
            lr_copy(u, other, me, other).start()
            return carry

        lax.fori_loop(1, count, lr_start, 0)
        begin = pl.multiple_of(me * (own * per_lr), own * per_lr)
        lr_in[u, me] = stage[pl.ds(begin, own * per_lr), :].astype(BF16)

        w_gate_t = jnp.transpose(w_gate[u].astype(F32)).astype(BF16)
        for i in range(rows):
            gate_t[i] = sigmoid(matmul(w_gate_t, zn_t[i]))

        def lr_wait(step, carry):
            other = lax.rem(me + step, count)
            lr_copy(u, me, other, other).wait_recv()
            return carry

        lax.fori_loop(1, count, lr_wait, 0)

        for c in range(0, own, 2):
            found = []
            for d in range(c, c + 2):
                both = lr_in[u, :, d * per_lr : (d + 1) * per_lr, :].astype(F32)
                left = both[:, :rows].reshape(n, n).astype(BF16)
                right = both[:, rows:].reshape(n, n).astype(BF16)
                contract = ((1,), (1,)) if u == 0 else ((0,), (0,))
                found.append(matmul(left, right, contract).reshape(count, rows, n))
            x_out[u, :, c * rows : (c + 2) * rows, :] = jnp.concatenate(found, axis=1).astype(BF16)

        def x_start(step, carry):
            other = lax.rem(me + step, count)
            x_copy(u, other, me, other).start()
            return carry

        lax.fori_loop(1, count, x_start, 0)
        x_in[u, me] = x_out[u, me]

        w_out_t = jnp.transpose(w_out[u].astype(F32)).astype(BF16)
        gain, bias = column(out_gain, u), column(out_bias, u)

        def x_wait(step, carry):
            other = lax.rem(me + step, count)
            x_copy(u, me, other, other).wait_recv()
            return carry

        lax.fori_loop(1, count, x_wait, 0)

        x = x_in[u].astype(F32).reshape(hidden, rows, n)
        mean = jnp.mean(x, axis=0)
        centred = x - mean[None]
        var = jnp.mean(centred * centred, axis=0)
        x_wide[...] = (centred * lax.rsqrt(var + 1e-05)[None]).reshape(hidden * rows, n)
        for i in range(rows):
            xn = (x_wide[pl.ds(i, hidden, stride=rows), :] * gain + bias).astype(BF16)
            z = z_t[i] + gate_t[i] * matmul(w_out_t, xn)
            if u == 0:
                z_t[i] = z.astype(BF16).astype(F32)
            else:
                out_ref[i] = jnp.transpose(z).astype(BF16)

        def drain(step, carry):
            other = lax.rem(me + step, count)
            lr_copy(u, other, me, other).wait_send()
            x_copy(u, other, me, other).wait_send()
            return carry

        lax.fori_loop(1, count, drain, 0)


def fused_call(count, pair, residue_mask, *params):
    rows, n, chans = pair.shape
    hidden = params[-1].shape[1]
    own = hidden // count
    vmem = pl.BlockSpec(memory_space=pltpu.VMEM)
    return pl.pallas_call(
        functools.partial(fused, count),
        out_shape=jax.ShapeDtypeStruct(pair.shape, BF16),
        in_specs=[vmem, vmem, pl.BlockSpec(memory_space=pltpu.SMEM)] + [vmem] * 7,
        out_specs=vmem,
        scratch_shapes=[
            pltpu.VMEM((rows, chans, n), F32),
            pltpu.VMEM((rows, chans, n), BF16),
            pltpu.VMEM((rows, chans, n), F32),
            pltpu.VMEM((hidden * 2 * rows, n), F32),
            pltpu.VMEM((2, count, own * 2 * rows, n), BF16),
            pltpu.VMEM((2, count, own * 2 * rows, n), BF16),
            pltpu.VMEM((2, count, own * rows, n), BF16),
            pltpu.VMEM((2, count, own * rows, n), BF16),
            pltpu.VMEM((hidden * rows, n), F32),
            pltpu.SemaphoreType.DMA((2, count)),
            pltpu.SemaphoreType.DMA((2, count)),
            pltpu.SemaphoreType.DMA((2, count)),
            pltpu.SemaphoreType.DMA((2, count)),
        ],
        compiler_params=pltpu.CompilerParams(
            collective_id=0, has_side_effects=True, vmem_limit_bytes=48 * 1024 * 1024
        ),
        cost_estimate=pl.CostEstimate(
            flops=4 * rows * n * chans * (5 * hidden + n + hidden),
            bytes_accessed=4 * rows * n * chans,
            transcendentals=6 * rows * n * hidden,
        ),
    )(pair, residue_mask.reshape(1, n), residue_mask, *params)


def per_device(count, fits, pair, *rest):
    rows, cols, chans = pair.shape
    hidden = rest[-1].shape[1]
    if (
        fits
        and rows == TILE
        and cols == rows * count == LANES
        and chans == LANES
        and hidden == LANES
        and hidden % (2 * count) == 0
    ):
        return fused_call(count, pair, *rest)
    return shards(pair, *rest)


def solution(mesh):
    in_specs = (P(("group", "row"), "col", None), P("group"), P(), P(), P(), P(), P(), P(), P())
    out_specs = P(("group", "row"), "col", None)
    body = functools.partial(per_device, mesh.shape["row"], mesh.shape["col"] == 1)
    return jax.shard_map(body, mesh=mesh, in_specs=in_specs, out_specs=out_specs, check_vma=False)
```

profile of v0, /device:TPU:25, one launch (start us, length us, event | category | flops | bytes accessed | tf_op | source)
XLA Modules:
  0.0 55.5 jit_solution(5581155406386563944)
XLA Ops:
  0.0 0.0 copy-start.8
  0.0 0.0 copy-start.4
  0.0 0.7 %copy-done.8 = s32[128]{0:T(128)S(1)} copy-done((s32[128]{0:T(128)S(1)}, s32[128]{0:T(128)}, u32[]{:S(2)}) %copy-start.8) | copy-done | bytes 536
  0.7 0.0 copy-done.4
  0.7 0.0 copy-start
  0.7 0.9 %copy-done = bf16[8,128,128]{2,1,0:T(8,128)(2,1)S(1)} copy-done((bf16[8,128,128]{2,1,0:T(8,128)(2,1)S(1)}, bf16[8,128,128]{2,1,0:T(8,128)(2,1)}, u32[]{:S(2)}) %copy-start) | copy-done | bytes 262168
  1.6 0.0 copy-start.1
  1.6 0.9 %copy-done.1 = bf16[2,128,512]{2,1,0:T(8,128)(2,1)S(1)} copy-done((bf16[2,128,512]{2,1,0:T(8,128)(2,1)S(1)}, bf16[2,128,512]{2,1,0:T(8,128)(2,1)}, u32[]{:S(2)}) %copy-start.1) | copy-done | bytes 262168
  2.6 0.0 copy-start.2
  2.6 0.8 %copy-done.2 = bf16[2,128,128]{2,1,0:T(8,128)(2,1)S(1)} copy-done((bf16[2,128,128]{2,1,0:T(8,128)(2,1)S(1)}, bf16[2,128,128]{2,1,0:T(8,128)(2,1)}, u32[]{:S(2)}) %copy-start.2) | copy-done | bytes 65560
  3.4 0.0 copy-start.3
  3.4 0.8 %copy-done.3 = bf16[2,128,128]{2,1,0:T(8,128)(2,1)S(1)} copy-done((bf16[2,128,128]{2,1,0:T(8,128)(2,1)S(1)}, bf16[2,128,128]{2,1,0:T(8,128)(2,1)}, u32[]{:S(2)}) %copy-start.3) | copy-done | bytes 65560
  4.3 0.0 copy-start.5
  4.3 0.7 %copy-done.5 = f32[2,128]{1,0:T(2,128)S(1)} copy-done((f32[2,128]{1,0:T(2,128)S(1)}, f32[2,128]{1,0:T(2,128)}, u32[]{:S(2)}) %copy-start.5) | copy-done | bytes 1048
  5.0 0.0 copy-start.6
  5.0 0.7 %copy-done.6 = f32[2,128]{1,0:T(2,128)S(1)} copy-done((f32[2,128]{1,0:T(2,128)S(1)}, f32[2,128]{1,0:T(2,128)}, u32[]{:S(2)}) %copy-start.6) | copy-done | bytes 1048
  5.6 0.0 copy-start.7
  5.6 0.7 %copy-done.7 = f32[2,128]{1,0:T(2,128)S(1)} copy-done((f32[2,128]{1,0:T(2,128)S(1)}, f32[2,128]{1,0:T(2,128)}, u32[]{:S(2)}) %copy-start.7) | copy-done | bytes 1048
  6.3 48.5 %shard_map.91 = bf16[8,128,128]{2,1,0:T(8,128)(2,1)S(1)} custom-call(bf16[8,128,128]{2,1,0:T(8,128)(2,1)S(1)} %copy-done, s32[1,128]{1,0:T(1,128)S(1)} %bitcast.1, s32[128]{0:T(128)S(1)} %copy-done.8, f32[2,128]{1,0:T(2,128)S(1)} %copy-done.4, f32[2,128]{1,0:T(2,128)S(1)} %copy-done.5, bf16[2,128,512]{2,1,0:T(8,128)(2,1)S(1)} %copy-done.1, ...), custom_call_target="tpu_custom_call" | custom-call | flops 469762048 | bytes 524288 | tf_op jit(solution)/shard_map/pallas_call | solution.py:286
  54.8 0.7 %copy.11 = bf16[8,128,128]{2,1,0:T(8,128)(2,1)} copy(bf16[8,128,128]{2,1,0:T(8,128)(2,1)S(1)} %shard_map.91) | data formatting | bytes 524288
Async XLA Ops:
  0.0 0.7 %copy-start.8 = (s32[128]{0:T(128)S(1)}, s32[128]{0:T(128)}, u32[]{:S(2)}) copy-start(s32[128]{0:T(128)} %mask_s.1) | copy-start | bytes 1540
  0.0 0.7 %copy-start.4 = (f32[2,128]{1,0:T(2,128)S(1)}, f32[2,128]{1,0:T(2,128)}, u32[]{:S(2)}) copy-start(f32[2,128]{1,0:T(2,128)} %ln_gain.1) | copy-start | bytes 3076
  0.7 0.9 %copy-start = (bf16[8,128,128]{2,1,0:T(8,128)(2,1)S(1)}, bf16[8,128,128]{2,1,0:T(8,128)(2,1)}, u32[]{:S(2)}) copy-start(bf16[8,128,128]{2,1,0:T(8,128)(2,1)} %pair_ref.1) | copy-start | bytes 786436
  1.6 0.9 %copy-start.1 = (bf16[2,128,512]{2,1,0:T(8,128)(2,1)S(1)}, bf16[2,128,512]{2,1,0:T(8,128)(2,1)}, u32[]{:S(2)}) copy-start(bf16[2,128,512]{2,1,0:T(8,128)(2,1)} %w_ab.1) | copy-start | bytes 786436
  2.6 0.8 %copy-start.2 = (bf16[2,128,128]{2,1,0:T(8,128)(2,1)S(1)}, bf16[2,128,128]{2,1,0:T(8,128)(2,1)}, u32[]{:S(2)}) copy-start(bf16[2,128,128]{2,1,0:T(8,128)(2,1)} %w_gate.1) | copy-start | bytes 196612
  3.4 0.8 %copy-start.3 = (bf16[2,128,128]{2,1,0:T(8,128)(2,1)S(1)}, bf16[2,128,128]{2,1,0:T(8,128)(2,1)}, u32[]{:S(2)}) copy-start(bf16[2,128,128]{2,1,0:T(8,128)(2,1)} %w_out.1) | copy-start | bytes 196612
  4.3 0.7 %copy-start.5 = (f32[2,128]{1,0:T(2,128)S(1)}, f32[2,128]{1,0:T(2,128)}, u32[]{:S(2)}) copy-start(f32[2,128]{1,0:T(2,128)} %ln_bias.1) | copy-start | bytes 3076
  5.0 0.7 %copy-start.6 = (f32[2,128]{1,0:T(2,128)S(1)}, f32[2,128]{1,0:T(2,128)}, u32[]{:S(2)}) copy-start(f32[2,128]{1,0:T(2,128)} %out_gain.1) | copy-start | bytes 3076
  5.6 0.7 %copy-start.7 = (f32[2,128]{1,0:T(2,128)S(1)}, f32[2,128]{1,0:T(2,128)}, u32[]{:S(2)}) copy-start(f32[2,128]{1,0:T(2,128)} %out_bias.1) | copy-start | bytes 3076
where the time goes:
time: 55.8 us; the launch traced here: 55.5 us
  Pallas kernels  48.5 us (87%)
  local copies, waits for them, and re-layouts  7.01 us (13%)
    pallas_call x1, Pallas kernels, fused_call(): pl.pallas_call(functools.partial(fused, count), out_shape=jax.ShapeDtypeS...  48.5 us
    unnamed x19, local copies, waits for them, and re-layouts  7.01 us

commit v1 on v0

--- a/solution.py
+++ b/solution.py
@@ -103,6 +103,7 @@
 BF16 = jnp.bfloat16
 TILE = 8
 LANES = 128
+PARTS = 1
 
 
 def sigmoid(v):
@@ -120,9 +121,18 @@
 
 def fused(
     count,
+    pair_hbm,
+    mask_hbm,
+    ln_gain_hbm,
+    ln_bias_hbm,
+    w_ab_hbm,
+    w_gate_hbm,
+    out_gain_hbm,
+    out_bias_hbm,
+    w_out_hbm,
+    out_ref,
     pair_ref,
     mask_ref,
-    mask_s,
     ln_gain,
     ln_bias,
     w_ab,
@@ -130,7 +140,7 @@
     out_gain,
     out_bias,
     w_out,
-    out_ref,
+    load_sem,
     z_t,
     zn_t,
     gate_t,
@@ -147,9 +157,30 @@
 ):
     rows, n, chans = pair_ref.shape
     hidden = w_out.shape[1]
-    own = hidden // count
+    half = hidden // PARTS
+    own = half // count
     per_lr = 2 * rows
+    wide = 2 * n
     me = lax.axis_index("row")
+
+    held = (pair_ref, mask_ref, ln_gain, ln_bias, w_ab, w_gate, out_gain, out_bias, w_out)
+    given = (
+        pair_hbm,
+        mask_hbm,
+        ln_gain_hbm,
+        ln_bias_hbm,
+        w_ab_hbm,
+        w_gate_hbm,
+        out_gain_hbm,
+        out_bias_hbm,
+        w_out_hbm,
+    )
+    loads = [
+        pltpu.make_async_copy(src, dst, load_sem.at[k])
+        for k, (src, dst) in enumerate(zip(given, held))
+    ]
+    for load in loads:
+        load.start()
 
     barrier = pltpu.get_barrier_semaphore()
 
@@ -160,158 +191,179 @@
         )
         return carry
 
-    lax.fori_loop(1, count, greet, 0)
-
-    def lr_copy(u, slot_out, slot_in, other):
+    lax.fori_loop(1, count, greet, 0, unroll=True)
+
+    others = pl.ds(0, count - 1)
+
+    def lr_copy(u, h, slot_out, slot_in, other):
         return pltpu.make_async_remote_copy(
-            src_ref=lr_out.at[u, slot_out],
-            dst_ref=lr_in.at[u, slot_in],
-            send_sem=lr_send.at[u, slot_out],
-            recv_sem=lr_recv.at[u, slot_in],
+            src_ref=lr_out.at[u, h, slot_out],
+            dst_ref=lr_in.at[u, h, slot_in],
+            send_sem=lr_send.at[u, h],
+            recv_sem=lr_recv.at[u, h],
             device_id={"row": other},
             device_id_type=pl.DeviceIdType.MESH,
         )
 
-    def x_copy(u, slot_out, slot_in, other):
+    def x_copy(u, h, slot_out, slot_in, other):
         return pltpu.make_async_remote_copy(
-            src_ref=x_out.at[u, slot_out],
-            dst_ref=x_in.at[u, slot_in],
-            send_sem=x_send.at[u, slot_out],
-            recv_sem=x_recv.at[u, slot_in],
+            src_ref=x_out.at[u, h, slot_out],
+            dst_ref=x_in.at[u, h, slot_in],
+            send_sem=x_send.at[u, h],
+            recv_sem=x_recv.at[u, h],
             device_id={"row": other},
             device_id_type=pl.DeviceIdType.MESH,
         )
 
+    for load in loads:
+        load.wait()
     mask_k = mask_ref[...].astype(F32)
+    lane = lax.broadcasted_iota(jnp.int32, mask_k.shape, 1)
+    masks = []
     for i in range(rows):
-        z_t[i] = jnp.transpose(pair_ref[i].astype(F32))
+        mine = jnp.sum(jnp.where(lane == me * rows + i, mask_k, 0.0), axis=1, keepdims=True)
+        masks.append(mask_k * mine)
+    pm = [jnp.concatenate(masks[i : i + 2], axis=1) for i in range(0, rows, 2)]
 
     for u in range(2):
         w_t = jnp.transpose(w_ab[u].astype(F32)).astype(BF16)
         gain, bias = column(ln_gain, u), column(ln_bias, u)
         for i in range(rows):
+            if u == 0:
+                z_t[i] = jnp.transpose(pair_ref[i].astype(F32))
             z = z_t[i]
             mean = jnp.mean(z, axis=0, keepdims=True)
             centred = z - mean
             var = jnp.mean(centred * centred, axis=0, keepdims=True)
-            zn = (centred * lax.rsqrt(var + 1e-05) * gain + bias).astype(BF16)
-            zn_t[i] = zn
-            proj = matmul(w_t, zn)
-            pm = mask_k * mask_s[me * rows + i].astype(F32)
-            left = sigmoid(proj[:hidden]) * proj[hidden : 2 * hidden] * pm
-            right = sigmoid(proj[2 * hidden : 3 * hidden]) * proj[3 * hidden :] * pm
-            stage[pl.ds(i, hidden, stride=per_lr), :] = left
-            stage[pl.ds(rows + i, hidden, stride=per_lr), :] = right
-
-        if u == 0:
-            pl.semaphore_wait(barrier, count - 1)
-
-        def lr_start(step, carry):
-            other = lax.rem(me + step, count)
-            begin = pl.multiple_of(other * (own * per_lr), own * per_lr)
-            lr_out[u, other] = stage[pl.ds(begin, own * per_lr), :].astype(BF16)
-            lr_copy(u, other, me, other).start()
-            return carry
-
-        lax.fori_loop(1, count, lr_start, 0)
-        begin = pl.multiple_of(me * (own * per_lr), own * per_lr)
-        lr_in[u, me] = stage[pl.ds(begin, own * per_lr), :].astype(BF16)
+            zn = centred * lax.rsqrt(var + 1e-05) * gain + bias
+            zn_t[:, i * n : (i + 1) * n] = zn.astype(BF16)
+
+        for h in range(PARTS):
+            w_h = jnp.concatenate(
+                [w_t[p * hidden + h * half : p * hidden + (h + 1) * half] for p in range(4)], axis=0
+            )
+            for i in range(0, rows, 2):
+                proj = matmul(w_h, zn_t[:, i * n : (i + 2) * n])
+                left = sigmoid(proj[:half]) * proj[half : 2 * half] * pm[i // 2]
+                right = sigmoid(proj[2 * half : 3 * half]) * proj[3 * half :] * pm[i // 2]
+                for d in range(2):
+                    at = h * half * per_lr + i + d
+                    stage[pl.ds(at, half, stride=per_lr), :] = left[:, d * n : (d + 1) * n]
+                    stage[pl.ds(at + rows, half, stride=per_lr), :] = right[:, d * n : (d + 1) * n]
+
+            if u == 0 and h == 0:
+                pl.semaphore_wait(barrier, count - 1)
+
+            def block(other):
+                begin = pl.multiple_of((h * half + other * own) * per_lr, own * per_lr)
+                return stage[pl.ds(begin, own * per_lr), :].astype(BF16)
+
+            def lr_start(step, carry):
+                other = lax.rem(me + step, count)
+                lr_out[u, h, other] = block(other)
+                lr_copy(u, h, other, me, other).start()
+                return carry
+
+            lax.fori_loop(1, count, lr_start, 0, unroll=True)
+            lr_in[u, h, me] = block(me)
 
         w_gate_t = jnp.transpose(w_gate[u].astype(F32)).astype(BF16)
-        for i in range(rows):
-            gate_t[i] = sigmoid(matmul(w_gate_t, zn_t[i]))
-
-        def lr_wait(step, carry):
-            other = lax.rem(me + step, count)
-            lr_copy(u, me, other, other).wait_recv()
-            return carry
-
-        lax.fori_loop(1, count, lr_wait, 0)
-
-        for c in range(0, own, 2):
-            found = []
-            for d in range(c, c + 2):
-                both = lr_in[u, :, d * per_lr : (d + 1) * per_lr, :].astype(F32)
-                left = both[:, :rows].reshape(n, n).astype(BF16)
-                right = both[:, rows:].reshape(n, n).astype(BF16)
-                contract = ((1,), (1,)) if u == 0 else ((0,), (0,))
-                found.append(matmul(left, right, contract).reshape(count, rows, n))
-            x_out[u, :, c * rows : (c + 2) * rows, :] = jnp.concatenate(found, axis=1).astype(BF16)
-
-        def x_start(step, carry):
-            other = lax.rem(me + step, count)
-            x_copy(u, other, me, other).start()
-            return carry
-
-        lax.fori_loop(1, count, x_start, 0)
-        x_in[u, me] = x_out[u, me]
-
+        for i in range(0, rows, 2):
+            at = slice(i * n, (i + 2) * n)
+            gate_t[:, at] = sigmoid(matmul(w_gate_t, zn_t[:, at]))
         w_out_t = jnp.transpose(w_out[u].astype(F32)).astype(BF16)
         gain, bias = column(out_gain, u), column(out_bias, u)
 
-        def x_wait(step, carry):
-            other = lax.rem(me + step, count)
-            x_copy(u, me, other, other).wait_recv()
-            return carry
-
-        lax.fori_loop(1, count, x_wait, 0)
+        for h in range(PARTS):
+
+            lr_copy(u, h, others, others, me).wait_recv()
+
+            for c in range(0, own, 2):
+                found = []
+                for d in range(c, c + 2):
+                    both = lr_in[u, h, :, d * per_lr : (d + 1) * per_lr, :].astype(F32)
+                    left = both[:, :rows].reshape(n, n).astype(BF16)
+                    right = both[:, rows:].reshape(n, n).astype(BF16)
+                    contract = ((1,), (1,)) if u == 0 else ((0,), (0,))
+                    found.append(matmul(left, right, contract).reshape(count, rows, n))
+                x_out[u, h, :, c * rows : (c + 2) * rows, :] = jnp.concatenate(
+                    found, axis=1
+                ).astype(BF16)
+
+            def x_start(step, carry):
+                other = lax.rem(me + step, count)
+                x_copy(u, h, other, me, other).start()
+                return carry
+
+            lax.fori_loop(1, count, x_start, 0, unroll=True)
+            x_in[u, h, me] = x_out[u, h, me]
+
+        for h in range(PARTS):
+
+            x_copy(u, h, others, others, me).wait_recv()
 
         x = x_in[u].astype(F32).reshape(hidden, rows, n)
         mean = jnp.mean(x, axis=0)
         centred = x - mean[None]
         var = jnp.mean(centred * centred, axis=0)
         x_wide[...] = (centred * lax.rsqrt(var + 1e-05)[None]).reshape(hidden * rows, n)
-        for i in range(rows):
-            xn = (x_wide[pl.ds(i, hidden, stride=rows), :] * gain + bias).astype(BF16)
-            z = z_t[i] + gate_t[i] * matmul(w_out_t, xn)
-            if u == 0:
-                z_t[i] = z.astype(BF16).astype(F32)
-            else:
-                out_ref[i] = jnp.transpose(z).astype(BF16)
-
-        def drain(step, carry):
-            other = lax.rem(me + step, count)
-            lr_copy(u, other, me, other).wait_send()
-            x_copy(u, other, me, other).wait_send()
-            return carry
-
-        lax.fori_loop(1, count, drain, 0)
+        for i in range(0, rows, 2):
+            xn = [
+                (x_wide[pl.ds(i + d, hidden, stride=rows), :] * gain + bias).astype(BF16)
+                for d in range(2)
+            ]
+            update = matmul(w_out_t, jnp.concatenate(xn, axis=1))
+            update = gate_t[:, i * n : (i + 2) * n] * update
+            for d in range(2):
+                z = z_t[i + d] + update[:, d * n : (d + 1) * n]
+                if u == 0:
+                    z_t[i + d] = z.astype(BF16).astype(F32)
+                else:
+                    out_ref[i + d] = jnp.transpose(z).astype(BF16)
+
+    for u in range(2):
+        for h in range(PARTS):
+
+            lr_copy(u, h, others, others, me).wait_send()
+            x_copy(u, h, others, others, me).wait_send()
 
 
 def fused_call(count, pair, residue_mask, *params):
     rows, n, chans = pair.shape
     hidden = params[-1].shape[1]
-    own = hidden // count
-    vmem = pl.BlockSpec(memory_space=pltpu.VMEM)
+    own = hidden // PARTS // count
+    args = (pair, residue_mask.reshape(1, n)) + params
     return pl.pallas_call(
         functools.partial(fused, count),
         out_shape=jax.ShapeDtypeStruct(pair.shape, BF16),
-        in_specs=[vmem, vmem, pl.BlockSpec(memory_space=pltpu.SMEM)] + [vmem] * 7,
-        out_specs=vmem,
-        scratch_shapes=[
+        in_specs=[pl.BlockSpec(memory_space=pltpu.HBM)] * len(args),
+        out_specs=pl.BlockSpec(memory_space=pltpu.VMEM),
+        scratch_shapes=[pltpu.VMEM(a.shape, a.dtype) for a in args]
+        + [
+            pltpu.SemaphoreType.DMA((len(args),)),
             pltpu.VMEM((rows, chans, n), F32),
-            pltpu.VMEM((rows, chans, n), BF16),
-            pltpu.VMEM((rows, chans, n), F32),
+            pltpu.VMEM((chans, rows * n), BF16),
+            pltpu.VMEM((chans, rows * n), F32),
             pltpu.VMEM((hidden * 2 * rows, n), F32),
-            pltpu.VMEM((2, count, own * 2 * rows, n), BF16),
-            pltpu.VMEM((2, count, own * 2 * rows, n), BF16),
-            pltpu.VMEM((2, count, own * rows, n), BF16),
-            pltpu.VMEM((2, count, own * rows, n), BF16),
+            pltpu.VMEM((2, PARTS, count, own * 2 * rows, n), BF16),
+            pltpu.VMEM((2, PARTS, count, own * 2 * rows, n), BF16),
+            pltpu.VMEM((2, PARTS, count, own * rows, n), BF16),
+            pltpu.VMEM((2, PARTS, count, own * rows, n), BF16),
             pltpu.VMEM((hidden * rows, n), F32),
-            pltpu.SemaphoreType.DMA((2, count)),
-            pltpu.SemaphoreType.DMA((2, count)),
-            pltpu.SemaphoreType.DMA((2, count)),
-            pltpu.SemaphoreType.DMA((2, count)),
+            pltpu.SemaphoreType.DMA((2, PARTS)),
+            pltpu.SemaphoreType.DMA((2, PARTS)),
+            pltpu.SemaphoreType.DMA((2, PARTS)),
+            pltpu.SemaphoreType.DMA((2, PARTS)),
         ],
         compiler_params=pltpu.CompilerParams(
-            collective_id=0, has_side_effects=True, vmem_limit_bytes=48 * 1024 * 1024
+            collective_id=0, has_side_effects=True, vmem_limit_bytes=63 * 1024 * 1024
         ),
         cost_estimate=pl.CostEstimate(
             flops=4 * rows * n * chans * (5 * hidden + n + hidden),
             bytes_accessed=4 * rows * n * chans,
             transcendentals=6 * rows * n * hidden,
         ),
-    )(pair, residue_mask.reshape(1, n), residue_mask, *params)
+    )(*args)
 
 
 def per_device(count, fits, pair, *rest):
@@ -323,7 +375,7 @@
         and cols == rows * count == LANES
         and chans == LANES
         and hidden == LANES
-        and hidden % (2 * count) == 0
+        and hidden % (2 * PARTS * count) == 0
     ):
         return fused_call(count, pair, *rest)
     return shards(pair, *rest)

time: 55.8 us -> 49 us (0.88)
  local copies, waits for them, and re-layouts: 7.01 us -> 1.67 us
  Pallas kernels: 48.5 us -> 47.1 us
    unnamed x19 -> x1, local copies, waits for them, and re-layouts: 7.01 us -> 1.67 us
    pallas_call x1, Pallas kernels: 48.5 us -> 47.1 us  [fused_call(): pl.pallas_call(functools.partial(fused, count), out_shape=jax.ShapeDtypeS...]
where the time goes in v1:
time: 49 us; the launch traced here: 48.8 us
  Pallas kernels  47.1 us (96%)
  local copies, waits for them, and re-layouts  1.67 us (3%)
    pallas_call x1, Pallas kernels, fused_call(): pl.pallas_call(functools.partial(fused, count), out_shape=jax.ShapeDtypeS...  47.1 us
    unnamed x1, local copies, waits for them, and re-layouts  1.67 us

profile of v1, /device:TPU:25, one launch (start us, length us, event | category | flops | bytes accessed | tf_op | source)
XLA Modules:
  0.0 48.8 jit_solution(2414108918489802252)
XLA Ops:
  0.0 47.1 %shard_map.91 = bf16[8,128,128]{2,1,0:T(8,128)(2,1)} custom-call(bf16[8,128,128]{2,1,0:T(8,128)(2,1)} %pair_hbm.1, s32[1,128]{1,0:T(1,128)} %bitcast.1, f32[2,128]{1,0:T(2,128)} %ln_gain_hbm.1, f32[2,128]{1,0:T(2,128)} %ln_bias_hbm.1, bf16[2,128,512]{2,1,0:T(8,128)(2,1)} %w_ab_hbm.1, bf16[2,128,128]{2,1,0:T(8,128)(2,1)} %w_gate_hbm.1, ...), custom_call_target="tpu_custom_call" | custom-call | flops 469762048 | bytes 524288 | tf_op jit(solution)/shard_map/pallas_call | solution.py:336
  47.2 1.7 %copy.11 = bf16[8,128,128]{2,1,0:T(8,128)(2,1)} copy(bf16[8,128,128]{2,1,0:T(8,128)(2,1)} %shard_map.91) | data formatting | bytes 524288

commit v2 on v1

--- a/solution.py
+++ b/solution.py
@@ -103,7 +103,6 @@
 BF16 = jnp.bfloat16
 TILE = 8
 LANES = 128
-PARTS = 1
 
 
 def sigmoid(v):
@@ -145,22 +144,28 @@
     zn_t,
     gate_t,
     stage,
-    lr_out,
-    lr_in,
-    x_out,
-    x_in,
+    w_next,
+    edges,
+    l_in0,
+    r_in0,
+    l_in1,
+    r_in1,
+    x_out0,
+    x_out1,
+    x_in0,
+    x_in1,
     x_wide,
-    lr_send,
-    lr_recv,
+    l_send,
+    l_recv,
+    r_send,
+    r_recv,
     x_send,
     x_recv,
 ):
     rows, n, chans = pair_ref.shape
     hidden = w_out.shape[1]
-    half = hidden // PARTS
-    own = half // count
-    per_lr = 2 * rows
-    wide = 2 * n
+    l_in, r_in = (l_in0, l_in1), (r_in0, r_in1)
+    x_out, x_in = (x_out0, x_out1), (x_in0, x_in1)
     me = lax.axis_index("row")
 
     held = (pair_ref, mask_ref, ln_gain, ln_bias, w_ab, w_gate, out_gain, out_bias, w_out)
@@ -193,27 +198,24 @@
 
     lax.fori_loop(1, count, greet, 0, unroll=True)
 
-    others = pl.ds(0, count - 1)
-
-    def lr_copy(u, h, slot_out, slot_in, other):
+    def send(src, dst, send_sem, recv_sem, other):
         return pltpu.make_async_remote_copy(
-            src_ref=lr_out.at[u, h, slot_out],
-            dst_ref=lr_in.at[u, h, slot_in],
-            send_sem=lr_send.at[u, h],
-            recv_sem=lr_recv.at[u, h],
+            src_ref=src,
+            dst_ref=dst,
+            send_sem=send_sem,
+            recv_sem=recv_sem,
             device_id={"row": other},
             device_id_type=pl.DeviceIdType.MESH,
         )
 
-    def x_copy(u, h, slot_out, slot_in, other):
-        return pltpu.make_async_remote_copy(
-            src_ref=x_out.at[u, h, slot_out],
-            dst_ref=x_in.at[u, h, slot_in],
-            send_sem=x_send.at[u, h],
-            recv_sem=x_recv.at[u, h],
-            device_id={"row": other},
-            device_id_type=pl.DeviceIdType.MESH,
-        )
+    def all_blocks(u, kind):
+        ref, send_sem, recv_sem = {
+            "l": (l_in[u], l_send, l_recv),
+            "r": (r_in[u], r_send, r_recv),
+            "x": (x_in[u], x_send, x_recv),
+        }[kind]
+        blocks = ref.at[pl.ds(0, ref.shape[0] - 1)]
+        return send(blocks, blocks, send_sem.at[u], recv_sem.at[u], me)
 
     for load in loads:
         load.wait()
@@ -226,7 +228,15 @@
     pm = [jnp.concatenate(masks[i : i + 2], axis=1) for i in range(0, rows, 2)]
 
     for u in range(2):
-        w_t = jnp.transpose(w_ab[u].astype(F32)).astype(BF16)
+        team = count // 2 if u == 0 else count
+        own = hidden // team
+        size = own * rows
+        member = lax.rem(me, team)
+        base = me - member
+        if u == 0:
+            w_t = jnp.transpose(w_ab[u].astype(F32)).astype(BF16)
+        else:
+            w_t = w_next[...]
         gain, bias = column(ln_gain, u), column(ln_bias, u)
         for i in range(rows):
             if u == 0:
@@ -238,34 +248,32 @@
             zn = centred * lax.rsqrt(var + 1e-05) * gain + bias
             zn_t[:, i * n : (i + 1) * n] = zn.astype(BF16)
 
-        for h in range(PARTS):
-            w_h = jnp.concatenate(
-                [w_t[p * hidden + h * half : p * hidden + (h + 1) * half] for p in range(4)], axis=0
-            )
-            for i in range(0, rows, 2):
-                proj = matmul(w_h, zn_t[:, i * n : (i + 2) * n])
-                left = sigmoid(proj[:half]) * proj[half : 2 * half] * pm[i // 2]
-                right = sigmoid(proj[2 * half : 3 * half]) * proj[3 * half :] * pm[i // 2]
-                for d in range(2):
-                    at = h * half * per_lr + i + d
-                    stage[pl.ds(at, half, stride=per_lr), :] = left[:, d * n : (d + 1) * n]
-                    stage[pl.ds(at + rows, half, stride=per_lr), :] = right[:, d * n : (d + 1) * n]
-
-            if u == 0 and h == 0:
-                pl.semaphore_wait(barrier, count - 1)
-
-            def block(other):
-                begin = pl.multiple_of((h * half + other * own) * per_lr, own * per_lr)
-                return stage[pl.ds(begin, own * per_lr), :].astype(BF16)
-
-            def lr_start(step, carry):
-                other = lax.rem(me + step, count)
-                lr_out[u, h, other] = block(other)
-                lr_copy(u, h, other, me, other).start()
-                return carry
-
-            lax.fori_loop(1, count, lr_start, 0, unroll=True)
-            lr_in[u, h, me] = block(me)
+        for i in range(0, rows, 2):
+            proj = matmul(w_t, zn_t[:, i * n : (i + 2) * n])
+            left = sigmoid(proj[:hidden]) * proj[hidden : 2 * hidden] * pm[i // 2]
+            right = sigmoid(proj[2 * hidden : 3 * hidden]) * proj[3 * hidden :] * pm[i // 2]
+            for d in range(2):
+                at = slice(d * n, (d + 1) * n)
+                stage[pl.ds(i + d, hidden, stride=rows), :] = left[:, at]
+                stage[pl.ds(hidden * rows + i + d, hidden, stride=rows), :] = right[:, at]
+        edges[u, 0] = stage[: hidden * rows, :].astype(BF16)
+        edges[u, 1] = stage[hidden * rows :, :].astype(BF16)
+
+        if u == 0:
+            pl.semaphore_wait(barrier, count - 1)
+
+        def block(side, device):
+            begin = pl.multiple_of(lax.rem(device, team) * size, size)
+            return edges.at[u, side, pl.ds(begin, size)]
+
+        for step in range(1, count):
+            other = lax.rem(me + step, count)
+            send(block(1, other), r_in[u].at[me], r_send.at[u], r_recv.at[u], other).start()
+            if step < team:
+                other = base + lax.rem(member + step, team)
+                send(block(0, other), l_in[u].at[member], l_send.at[u], l_recv.at[u], other).start()
+        r_in[u][me] = block(1, me)[...]
+        l_in[u][member] = block(0, me)[...]
 
         w_gate_t = jnp.transpose(w_gate[u].astype(F32)).astype(BF16)
         for i in range(0, rows, 2):
@@ -273,36 +281,33 @@
             gate_t[:, at] = sigmoid(matmul(w_gate_t, zn_t[:, at]))
         w_out_t = jnp.transpose(w_out[u].astype(F32)).astype(BF16)
         gain, bias = column(out_gain, u), column(out_bias, u)
-
-        for h in range(PARTS):
-
-            lr_copy(u, h, others, others, me).wait_recv()
-
-            for c in range(0, own, 2):
-                found = []
-                for d in range(c, c + 2):
-                    both = lr_in[u, h, :, d * per_lr : (d + 1) * per_lr, :].astype(F32)
-                    left = both[:, :rows].reshape(n, n).astype(BF16)
-                    right = both[:, rows:].reshape(n, n).astype(BF16)
-                    contract = ((1,), (1,)) if u == 0 else ((0,), (0,))
-                    found.append(matmul(left, right, contract).reshape(count, rows, n))
-                x_out[u, h, :, c * rows : (c + 2) * rows, :] = jnp.concatenate(
-                    found, axis=1
-                ).astype(BF16)
-
-            def x_start(step, carry):
-                other = lax.rem(me + step, count)
-                x_copy(u, h, other, me, other).start()
-                return carry
-
-            lax.fori_loop(1, count, x_start, 0, unroll=True)
-            x_in[u, h, me] = x_out[u, h, me]
-
-        for h in range(PARTS):
-
-            x_copy(u, h, others, others, me).wait_recv()
-
-        x = x_in[u].astype(F32).reshape(hidden, rows, n)
+        if u == 0:
+            w_next[...] = jnp.transpose(w_ab[1].astype(F32)).astype(BF16)
+
+        all_blocks(u, "l").wait_recv()
+        all_blocks(u, "r").wait_recv()
+        for c in range(0, own, 2):
+            at = slice(c * rows, (c + 2) * rows)
+            lefts = l_in[u][:, at, :].astype(F32)
+            rights = r_in[u][:, at, :].astype(F32)
+            found = []
+            for d in range(2):
+                at_d = slice(d * rows, (d + 1) * rows)
+                left = lefts[:, at_d].reshape(team * rows, n).astype(BF16)
+                right = rights[:, at_d].reshape(n, n).astype(BF16)
+                contract = ((1,), (1,)) if u == 0 else ((0,), (0,))
+                found.append(matmul(left, right, contract).reshape(team, rows, n))
+            x_out[u][:, at, :] = jnp.concatenate(found, axis=1).astype(BF16)
+
+        for step in range(1, team):
+            to = lax.rem(member + step, team)
+            send(
+                x_out[u].at[to], x_in[u].at[member], x_send.at[u], x_recv.at[u], base + to
+            ).start()
+        x_in[u][member] = x_out[u][member]
+        all_blocks(u, "x").wait_recv()
+
+        x = x_in[u][...].astype(F32).reshape(hidden, rows, n)
         mean = jnp.mean(x, axis=0)
         centred = x - mean[None]
         var = jnp.mean(centred * centred, axis=0)
@@ -322,16 +327,14 @@
                     out_ref[i + d] = jnp.transpose(z).astype(BF16)
 
     for u in range(2):
-        for h in range(PARTS):
-
-            lr_copy(u, h, others, others, me).wait_send()
-            x_copy(u, h, others, others, me).wait_send()
+        for kind in ("l", "r", "x"):
+            all_blocks(u, kind).wait_send()
 
 
 def fused_call(count, pair, residue_mask, *params):
     rows, n, chans = pair.shape
     hidden = params[-1].shape[1]
-    own = hidden // PARTS // count
+    per = rows * hidden // count
     args = (pair, residue_mask.reshape(1, n)) + params
     return pl.pallas_call(
         functools.partial(fused, count),
@@ -345,15 +348,23 @@
             pltpu.VMEM((chans, rows * n), BF16),
             pltpu.VMEM((chans, rows * n), F32),
             pltpu.VMEM((hidden * 2 * rows, n), F32),
-            pltpu.VMEM((2, PARTS, count, own * 2 * rows, n), BF16),
-            pltpu.VMEM((2, PARTS, count, own * 2 * rows, n), BF16),
-            pltpu.VMEM((2, PARTS, count, own * rows, n), BF16),
-            pltpu.VMEM((2, PARTS, count, own * rows, n), BF16),
+            pltpu.VMEM((4 * hidden, chans), BF16),
+            pltpu.VMEM((2, 2, hidden * rows, n), BF16),
+            pltpu.VMEM((count // 2, 2 * per, n), BF16),
+            pltpu.VMEM((count, 2 * per, n), BF16),
+            pltpu.VMEM((count, per, n), BF16),
+            pltpu.VMEM((count, per, n), BF16),
+            pltpu.VMEM((count // 2, 2 * per, n), BF16),
+            pltpu.VMEM((count, per, n), BF16),
+            pltpu.VMEM((count // 2, 2 * per, n), BF16),
+            pltpu.VMEM((count, per, n), BF16),
             pltpu.VMEM((hidden * rows, n), F32),
-            pltpu.SemaphoreType.DMA((2, PARTS)),
-            pltpu.SemaphoreType.DMA((2, PARTS)),
-            pltpu.SemaphoreType.DMA((2, PARTS)),
-            pltpu.SemaphoreType.DMA((2, PARTS)),
+            pltpu.SemaphoreType.DMA((2,)),
+            pltpu.SemaphoreType.DMA((2,)),
+            pltpu.SemaphoreType.DMA((2,)),
+            pltpu.SemaphoreType.DMA((2,)),
+            pltpu.SemaphoreType.DMA((2,)),
+            pltpu.SemaphoreType.DMA((2,)),
         ],
         compiler_params=pltpu.CompilerParams(
             collective_id=0, has_side_effects=True, vmem_limit_bytes=63 * 1024 * 1024
@@ -375,7 +386,8 @@
         and cols == rows * count == LANES
         and chans == LANES
         and hidden == LANES
-        and hidden % (2 * PARTS * count) == 0
+        and hidden % (2 * count) == 0
+        and count % 2 == 0
     ):
         return fused_call(count, pair, *rest)
     return shards(pair, *rest)

time: 49 us -> 47.6 us (0.971); the launches traced: 48.8 us -> 46.8 us
  Pallas kernels: 47.1 us -> 45.2 us
    pallas_call x1, Pallas kernels: 47.1 us -> 45.2 us  [fused_call(): pl.pallas_call(functools.partial(fused, count), out_shape=jax.ShapeDtypeS...]
where the time goes in v2:
time: 47.6 us; the launch traced here: 46.8 us
  Pallas kernels  45.2 us (95%)
  local copies, waits for them, and re-layouts  1.67 us (4%)
    pallas_call x1, Pallas kernels, fused_call(): pl.pallas_call(functools.partial(fused, count), out_shape=jax.ShapeDtypeS...  45.2 us
    unnamed x1, local copies, waits for them, and re-layouts  1.67 us

profile of v2, /device:TPU:25, one launch (start us, length us, event | category | flops | bytes accessed | tf_op | source)
XLA Modules:
  0.0 46.8 jit_solution(12680798999114958660)
XLA Ops:
  0.0 45.2 %shard_map.91 = bf16[8,128,128]{2,1,0:T(8,128)(2,1)} custom-call(bf16[8,128,128]{2,1,0:T(8,128)(2,1)} %pair_hbm.1, s32[1,128]{1,0:T(1,128)} %bitcast.1, f32[2,128]{1,0:T(2,128)} %ln_gain_hbm.1, f32[2,128]{1,0:T(2,128)} %ln_bias_hbm.1, bf16[2,128,512]{2,1,0:T(8,128)(2,1)} %w_ab_hbm.1, bf16[2,128,128]{2,1,0:T(8,128)(2,1)} %w_gate_hbm.1, ...), custom_call_target="tpu_custom_call" | custom-call | flops 469762048 | bytes 524288 | tf_op jit(solution)/shard_map/pallas_call | solution.py:339
  45.2 1.7 %copy.11 = bf16[8,128,128]{2,1,0:T(8,128)(2,1)} copy(bf16[8,128,128]{2,1,0:T(8,128)(2,1)} %shard_map.91) | data formatting | bytes 524288

commit v3 on v2

--- a/solution.py
+++ b/solution.py
@@ -145,26 +145,25 @@
     gate_t,
     stage,
     w_next,
-    edges,
-    l_in0,
-    r_in0,
-    l_in1,
-    r_in1,
+    edges0,
+    edges1,
+    in0,
+    in1,
     x_out0,
     x_out1,
     x_in0,
     x_in1,
     x_wide,
-    l_send,
-    l_recv,
-    r_send,
-    r_recv,
+    near_send,
+    near_recv,
+    far_send,
+    far_recv,
     x_send,
     x_recv,
 ):
     rows, n, chans = pair_ref.shape
     hidden = w_out.shape[1]
-    l_in, r_in = (l_in0, l_in1), (r_in0, r_in1)
+    edges, edges_in = (edges0, edges1), (in0, in1)
     x_out, x_in = (x_out0, x_out1), (x_in0, x_in1)
     me = lax.axis_index("row")
 
@@ -209,13 +208,14 @@
         )
 
     def all_blocks(u, kind):
-        ref, send_sem, recv_sem = {
-            "l": (l_in[u], l_send, l_recv),
-            "r": (r_in[u], r_send, r_recv),
-            "x": (x_in[u], x_send, x_recv),
-        }[kind]
-        blocks = ref.at[pl.ds(0, ref.shape[0] - 1)]
-        return send(blocks, blocks, send_sem.at[u], recv_sem.at[u], me)
+        if kind == "x":
+            blocks = x_in[u].at[pl.ds(0, x_in[u].shape[0] - 1)]
+            return send(blocks, blocks, x_send.at[u], x_recv.at[u], me)
+        if kind == "near":
+            blocks = edges_in[u].at[pl.ds(0, edges[u].shape[0] - 1)]
+            return send(blocks, blocks, near_send.at[u], near_recv.at[u], me)
+        blocks = edges_in[u].at[pl.ds(0, count - edges[u].shape[0]), 1]
+        return send(blocks, blocks, far_send, far_recv, me)
 
     for load in loads:
         load.wait()
@@ -256,24 +256,27 @@
                 at = slice(d * n, (d + 1) * n)
                 stage[pl.ds(i + d, hidden, stride=rows), :] = left[:, at]
                 stage[pl.ds(hidden * rows + i + d, hidden, stride=rows), :] = right[:, at]
-        edges[u, 0] = stage[: hidden * rows, :].astype(BF16)
-        edges[u, 1] = stage[hidden * rows :, :].astype(BF16)
+        half = hidden * rows
+        edges[u][:, 0] = stage[:half, :].astype(BF16).reshape(team, size, n)
+        edges[u][:, 1] = stage[half:, :].astype(BF16).reshape(team, size, n)
 
         if u == 0:
             pl.semaphore_wait(barrier, count - 1)
 
-        def block(side, device):
-            begin = pl.multiple_of(lax.rem(device, team) * size, size)
-            return edges.at[u, side, pl.ds(begin, size)]
-
-        for step in range(1, count):
-            other = lax.rem(me + step, count)
-            send(block(1, other), r_in[u].at[me], r_send.at[u], r_recv.at[u], other).start()
-            if step < team:
-                other = base + lax.rem(member + step, team)
-                send(block(0, other), l_in[u].at[member], l_send.at[u], l_recv.at[u], other).start()
-        r_in[u][me] = block(1, me)[...]
-        l_in[u][member] = block(0, me)[...]
+        for step in range(1, team):
+            to = lax.rem(member + step, team)
+            near = edges_in[u].at[me]
+            send(edges[u].at[to], near, near_send.at[u], near_recv.at[u], base + to).start()
+            if team < count:
+                to = lax.rem(member + step, team)
+                far = edges_in[u].at[me, 1]
+                other = lax.rem(base + team + to, count)
+                send(edges[u].at[to, 1], far, far_send, far_recv, other).start()
+        if team < count:
+            far = edges_in[u].at[me, 1]
+            other = lax.rem(me + team, count)
+            send(edges[u].at[member, 1], far, far_send, far_recv, other).start()
+        edges_in[u][me] = edges[u][member]
 
         w_gate_t = jnp.transpose(w_gate[u].astype(F32)).astype(BF16)
         for i in range(0, rows, 2):
@@ -284,12 +287,13 @@
         if u == 0:
             w_next[...] = jnp.transpose(w_ab[1].astype(F32)).astype(BF16)
 
-        all_blocks(u, "l").wait_recv()
-        all_blocks(u, "r").wait_recv()
+        all_blocks(u, "near").wait_recv()
+        if team < count:
+            all_blocks(u, "far").wait_recv()
         for c in range(0, own, 2):
             at = slice(c * rows, (c + 2) * rows)
-            lefts = l_in[u][:, at, :].astype(F32)
-            rights = r_in[u][:, at, :].astype(F32)
+            lefts = edges_in[u][pl.ds(base, team), 0, at, :].astype(F32)
+            rights = edges_in[u][:, 1, at, :].astype(F32)
             found = []
             for d in range(2):
                 at_d = slice(d * rows, (d + 1) * rows)
@@ -327,8 +331,9 @@
                     out_ref[i + d] = jnp.transpose(z).astype(BF16)
 
     for u in range(2):
-        for kind in ("l", "r", "x"):
+        for kind in ("near", "x"):
             all_blocks(u, kind).wait_send()
+    all_blocks(0, "far").wait_send()
 
 
 def fused_call(count, pair, residue_mask, *params):
@@ -349,11 +354,10 @@
             pltpu.VMEM((chans, rows * n), F32),
             pltpu.VMEM((hidden * 2 * rows, n), F32),
             pltpu.VMEM((4 * hidden, chans), BF16),
-            pltpu.VMEM((2, 2, hidden * rows, n), BF16),
-            pltpu.VMEM((count // 2, 2 * per, n), BF16),
-            pltpu.VMEM((count, 2 * per, n), BF16),
-            pltpu.VMEM((count, per, n), BF16),
-            pltpu.VMEM((count, per, n), BF16),
+            pltpu.VMEM((count // 2, 2, 2 * per, n), BF16),
+            pltpu.VMEM((count, 2, per, n), BF16),
+            pltpu.VMEM((count, 2, 2 * per, n), BF16),
+            pltpu.VMEM((count, 2, per, n), BF16),
             pltpu.VMEM((count // 2, 2 * per, n), BF16),
             pltpu.VMEM((count, per, n), BF16),
             pltpu.VMEM((count // 2, 2 * per, n), BF16),
@@ -361,8 +365,8 @@
             pltpu.VMEM((hidden * rows, n), F32),
             pltpu.SemaphoreType.DMA((2,)),
             pltpu.SemaphoreType.DMA((2,)),
-            pltpu.SemaphoreType.DMA((2,)),
-            pltpu.SemaphoreType.DMA((2,)),
+            pltpu.SemaphoreType.DMA,
+            pltpu.SemaphoreType.DMA,
             pltpu.SemaphoreType.DMA((2,)),
             pltpu.SemaphoreType.DMA((2,)),
         ],

time: 47.6 us -> 46.5 us (0.977); the launches traced: 46.8 us -> 46.3 us
  Pallas kernels: 45.2 us -> 44.6 us
    pallas_call x1, Pallas kernels: 45.2 us -> 44.6 us  [fused_call(): pl.pallas_call(functools.partial(fused, count), out_shape=jax.ShapeDtypeS...]
where the time goes in v3:
time: 46.5 us; the launch traced here: 46.3 us
  Pallas kernels  44.6 us (96%)
  local copies, waits for them, and re-layouts  1.67 us (4%)
    pallas_call x1, Pallas kernels, fused_call(): pl.pallas_call(functools.partial(fused, count), out_shape=jax.ShapeDtypeS...  44.6 us
    unnamed x1, local copies, waits for them, and re-layouts  1.67 us

profile of v3, /device:TPU:25, one launch (start us, length us, event | category | flops | bytes accessed | tf_op | source)
XLA Modules:
  0.0 46.3 jit_solution(15955668901308519300)
XLA Ops:
  0.0 44.6 %shard_map.91 = bf16[8,128,128]{2,1,0:T(8,128)(2,1)} custom-call(bf16[8,128,128]{2,1,0:T(8,128)(2,1)} %pair_hbm.1, s32[1,128]{1,0:T(1,128)} %bitcast.1, f32[2,128]{1,0:T(2,128)} %ln_gain_hbm.1, f32[2,128]{1,0:T(2,128)} %ln_bias_hbm.1, bf16[2,128,512]{2,1,0:T(8,128)(2,1)} %w_ab_hbm.1, bf16[2,128,128]{2,1,0:T(8,128)(2,1)} %w_gate_hbm.1, ...), custom_call_target="tpu_custom_call" | custom-call | flops 469762048 | bytes 524288 | tf_op jit(solution)/shard_map/pallas_call | solution.py:344
  44.6 1.7 %copy.11 = bf16[8,128,128]{2,1,0:T(8,128)(2,1)} copy(bf16[8,128,128]{2,1,0:T(8,128)(2,1)} %shard_map.91) | data formatting | bytes 524288

commit v4 on v3

--- a/solution.py
+++ b/solution.py
@@ -217,7 +217,7 @@
         blocks = edges_in[u].at[pl.ds(0, count - edges[u].shape[0]), 1]
         return send(blocks, blocks, far_send, far_recv, me)
 
-    for load in loads:
+    for load in loads[:5]:
         load.wait()
     mask_k = mask_ref[...].astype(F32)
     lane = lax.broadcasted_iota(jnp.int32, mask_k.shape, 1)
@@ -278,6 +278,9 @@
             send(edges[u].at[member, 1], far, far_send, far_recv, other).start()
         edges_in[u][me] = edges[u][member]
 
+        if u == 0:
+            for load in loads[5:]:
+                load.wait()
         w_gate_t = jnp.transpose(w_gate[u].astype(F32)).astype(BF16)
         for i in range(0, rows, 2):
             at = slice(i * n, (i + 2) * n)

time: 46.5 us -> 46.5 us (level)
  no operation moved by 1% of the time
where the time goes in v4:
time: 46.5 us; the launch traced here: 46.3 us
  Pallas kernels  44.6 us (96%)
  local copies, waits for them, and re-layouts  1.67 us (4%)
    pallas_call x1, Pallas kernels, fused_call(): pl.pallas_call(functools.partial(fused, count), out_shape=jax.ShapeDtypeS...  44.6 us
    unnamed x1, local copies, waits for them, and re-layouts  1.67 us

profile of v4, /device:TPU:25, one launch (start us, length us, event | category | flops | bytes accessed | tf_op | source)
XLA Modules:
  0.0 46.3 jit_solution(9632137683009759934)
XLA Ops:
  0.0 44.6 %shard_map.91 = bf16[8,128,128]{2,1,0:T(8,128)(2,1)} custom-call(bf16[8,128,128]{2,1,0:T(8,128)(2,1)} %pair_hbm.1, s32[1,128]{1,0:T(1,128)} %bitcast.1, f32[2,128]{1,0:T(2,128)} %ln_gain_hbm.1, f32[2,128]{1,0:T(2,128)} %ln_bias_hbm.1, bf16[2,128,512]{2,1,0:T(8,128)(2,1)} %w_ab_hbm.1, bf16[2,128,128]{2,1,0:T(8,128)(2,1)} %w_gate_hbm.1, ...), custom_call_target="tpu_custom_call" | custom-call | flops 469762048 | bytes 524288 | tf_op jit(solution)/shard_map/pallas_call | solution.py:347
  44.7 1.7 %copy.11 = bf16[8,128,128]{2,1,0:T(8,128)(2,1)} copy(bf16[8,128,128]{2,1,0:T(8,128)(2,1)} %shard_map.91) | data formatting | bytes 524288
